TPU v7x, 512 devices: a whole 4x8x8 slice. The times are simulated.
512 devices in a mesh: cluster: 32 (over z_hi, x, core), blk: 16 (over y, z_lo).
Axes of the slice: x: 4, y: 8, z: 8 (z_hi: 4, z_lo: 2; z = z_hi * 2 + z_lo), core: 2. Of those that a mesh axis runs over, the one named last changes fastest.
Arguments:
- coeff: bfloat16 [1024, 8, 2048], P('cluster', None, 'blk'), may hold values from -0.375 to 0.375
- intersection: int32 [32, 32], replicated, may hold values from 0 to 1023, as said below
- basis_vals: bfloat16 [131072, 256], P(('cluster', 'blk')), may hold values from -6 to 6
- coulomb: bfloat16 [131072, 7, 256], P(('cluster', 'blk')), may hold values from -0.125 to 0.125
- reach: int32 [512], P(('cluster', 'blk')), may hold values from 0 to 3, as said below
Outputs:
- exchange_out: bfloat16 [131072, 2048], P(('cluster', 'blk'))
Inputs may be any that keep to these rules, and one draw needn't show every extreme that they name: `intersection`: each row lists 32 distinct atoms; atom a is owned by cluster a // 32; at most 2 atoms of one row have the same owner, and each row c holds exactly 2 atoms owned by cluster c. `reach`: some block reaches 3 and some block reaches 0.
All inputs are finite; a program needn't handle non-finite values.
Results may differ from a plain program's by a relative error of at most 0.0059.
Values may be sent and summed in bfloat16 or wider, within the bound.
A program may use at most 64 MiB of HBM per device.

v0:
```python
import jax
import jax.numpy as jnp
from jax import lax
from jax.sharding import PartitionSpec as P


def passed_along(value, axis, steps):
    count = lax.axis_size(axis)
    pairs = [(source, (source + steps) % count) for source in range(count)]
    return lax.ppermute(value, axis, pairs)


def block_term(local_vals, source, coul_tile, within, norm_factor):
    density = (
        lax.dot_general(
            local_vals, source, (((1,), (1,)), ((), ())), preferred_element_type=jnp.float32
        )
        * norm_factor
    )
    masked_tile = jnp.where(
        within, density * coul_tile.astype(jnp.float32), jnp.float32(0.0)
    ).astype(jnp.bfloat16)
    return jnp.dot(masked_tile, source, preferred_element_type=jnp.float32)


def on_device(coeff, intersection, basis_vals, coulomb, reach):
    num_clusters = lax.axis_size("cluster")
    my_cluster = lax.axis_index("cluster")
    atom_count = coeff.shape[0]
    list_len = intersection.shape[1]
    capacity = 2 * list_len // num_clusters
    num_funcs = coeff.shape[1]
    my_columns = coeff.shape[2]
    half_stops = (coulomb.shape[1] - 1) // 2
    owners = intersection // atom_count
    same_owner = owners[:, :, None] == owners[:, None, :]
    earlier = jnp.arange(list_len)[None, :] < jnp.arange(list_len)[:, None]
    slot_rank = jnp.sum(jnp.logical_and(same_owner, earlier[None, :, :]).astype(jnp.int32), axis=2)
    matches = jnp.logical_and(
        (owners == my_cluster)[:, :, None],
        slot_rank[:, :, None] == jnp.arange(capacity)[None, None, :],
    )
    local_atom = intersection - my_cluster * atom_count
    source_rows = jnp.sum(jnp.where(matches, local_atom[:, :, None], 0), axis=1)
    filled = jnp.any(matches, axis=1)
    outgoing = jnp.take(coeff, source_rows.reshape(-1), axis=0)
    outgoing = jnp.where(filled.reshape(-1)[:, None, None], outgoing, jnp.zeros_like(outgoing))
    outgoing = outgoing.reshape(num_clusters, capacity, num_funcs, my_columns)
    incoming = lax.all_to_all(outgoing, "cluster", split_axis=0, concat_axis=0, tiled=True)
    my_owners = lax.dynamic_index_in_dim(owners, my_cluster, 0, keepdims=False)
    my_ranks = lax.dynamic_index_in_dim(slot_rank, my_cluster, 0, keepdims=False)
    positions = my_owners * capacity + my_ranks
    needed = jnp.take(
        incoming.reshape(num_clusters * capacity, num_funcs * my_columns), positions, axis=0
    )
    needed = needed.reshape(list_len * num_funcs, my_columns)
    local_vals = jnp.dot(
        basis_vals,
        lax.all_gather(needed, "blk", axis=1, tiled=True),
        preferred_element_type=jnp.float32,
    ).astype(jnp.bfloat16)
    norm_factor = local_vals.shape[1] ** (-0.5)
    my_reach = reach[0]

    def term(source, offset):
        return block_term(
            local_vals,
            source,
            coulomb[:, offset + half_stops, :],
            abs(offset) <= my_reach,
            norm_factor,
        )

    accumulated = term(local_vals, 0)
    upward = local_vals
    downward = local_vals
    for stop_num in range(1, half_stops + 1):
        upward = passed_along(upward, "blk", -1)
        accumulated = accumulated + term(upward, stop_num)
        downward = passed_along(downward, "blk", 1)
        accumulated = accumulated + term(downward, -stop_num)
    return accumulated.astype(jnp.bfloat16)


def solution(mesh):
    return jax.shard_map(
        on_device,
        mesh=mesh,
        in_specs=(
            P("cluster", None, "blk"),
            P(),
            P(("cluster", "blk"), None),
            P(("cluster", "blk"), None, None),
            P(("cluster", "blk")),
        ),
        out_specs=P(("cluster", "blk"), None),
        check_vma=False,
    )
```

profile of v0, /device:TPU:114, one launch (start us, length us, event | category | flops | bytes accessed | tf_op | source)
XLA Modules:
  0.0 255.3 jit_solution(13018517774100364596)
XLA Ops:
  6.5 0.0 copy-start
  6.5 0.8 broadcast_compare_fusion
  7.3 0.7 broadcast_subtract_fusion
  8.0 0.8 convert_reduce_fusion
  8.8 0.1 select_reduce_fusion
  8.9 0.1 copy.8
  9.0 0.1 fusion.70
  9.2 0.1 reshape.131
  9.3 0.1 copy.7
  9.4 0.1 copy.6
  9.5 1.5 gather_fusion
  11.0 0.9 select_select_fusion
  11.8 12.6 %all-to-all-start = ((bf16[32,2,8,128]{3,2,1,0:T(8,128)(2,1)}), bf16[32,2,8,128]{3,2,1,0:T(8,128)(2,1)S(1)}, u32[]{:S(2)}, u32[]{:S(2)}) async-start(bf16[32,2,8,128]{3,2,1,0:T(8,128)(2,1)} %select_select_fusion), calls=%async_computation | async-start | bytes 262144 | tf_op jit(solution)/shard_map/all_to_all | solution.py:49
  24.4 0.0 all-gather.2.cloned.1.call-start
  24.5 0.1 broadcast_in_dim.66
  24.5 0.1 broadcast_in_dim.67
  24.7 9.1 %all-to-all-done = bf16[32,2,8,128]{3,2,1,0:T(8,128)(2,1)S(1)} async-done(((bf16[32,2,8,128]{3,2,1,0:T(8,128)(2,1)}), bf16[32,2,8,128]{3,2,1,0:T(8,128)(2,1)S(1)}, u32[]{:S(2)}, u32[]{:S(2)}) %all-to-all-start) | async-done | bytes 131104 | tf_op jit(solution)/shard_map/all_to_all | solution.py:49
  33.8 0.6 gather_fusion.1
  34.4 0.7 broadcast_select_fusion
  35.2 0.0 all-gather.2.cloned.1.call-update
  35.2 77.8 %all-gather.2.cloned.1.call-done = bf16[256,2048]{1,0:T(8,128)(2,1)} async-done(((bf16[256,128]{1,0:T(8,128)(2,1)}), bf16[256,2048]{1,0:T(8,128)(2,1)}) %all-gather.2.cloned.1.call-update) | async-done | bytes 1048592 | tf_op jit(solution)/shard_map/all_gather | solution.py:59
  113.0 0.0 copy-done
  113.0 1.7 convolution_convert_fusion
  114.7 1.9 collective-permute-start.1
  116.6 3.9 %collective-permute-start = (bf16[256,2048]{0,1:T(8,128)(2,1)S(1)}, bf16[256,2048]{0,1:T(8,128)(2,1)}, u32[]{:S(2)}, u32[]{:S(2)}) collective-permute-start(bf16[256,2048]{0,1:T(8,128)(2,1)S(1)} %bitcast.85), channel_id=1, source_target_pairs={{0,15},{1,0},{2,1},{3,2},{4,3},{5,4},{6,5},{7,6},{8,7},{9,8},{10,9... | collective-permute-start | bytes 3145736 | tf_op jit(solution)/shard_map/ppermute | solution.py:10
  120.5 41.8 %collective-permute-done.1 = bf16[256,2048]{0,1:T(8,128)(2,1)} collective-permute-done((bf16[256,2048]{0,1:T(8,128)(2,1)S(1)}, bf16[256,2048]{0,1:T(8,128)(2,1)}, u32[]{:S(2)}, u32[]{:S(2)}) %collective-permute-start.1) | collective-permute-done | bytes 1048608 | tf_op jit(solution)/shard_map/ppermute | solution.py:10
  162.3 1.9 collective-permute-start.3
  164.9 0.0 collective-permute-done
  164.9 3.9 %collective-permute-start.2 = (bf16[256,2048]{0,1:T(8,128)(2,1)}, bf16[256,2048]{0,1:T(8,128)(2,1)}, u32[]{:S(2)}, u32[]{:S(2)}) collective-permute-start(bf16[256,2048]{0,1:T(8,128)(2,1)} %collective-permute-done), channel_id=1, source_target_pairs={{0,15},{1,0},{2,1},{3,2},{4,3},{5,4},{6,5},{7,6},{8,7},{9,8},{10,9... | collective-permute-start | bytes 3145736 | tf_op jit(solution)/shard_map/ppermute | solution.py:10
  168.9 2.2 fusion.26
  171.1 4.4 %convolution_add_fusion.3 = f32[256,2048]{1,0:T(8,128)} fusion(f32[256,2048]{1,0:T(8,128)S(1)} %fusion.26, bf16[256,2048]{0,1:T(8,128)(2,1)} %collective-permute-done, bf16[2048,256]{1,0:T(8,128)(2,1)S(1)} %convolution_convert_fusion, bf16[256,7,256]{2,0,1:T(8,128)(2,1)} %param.8, pred[]{:T(512)} %bitcast.7), kind=kOutput, calls=%fused_computation.7 | convolution fusion | flops 537722880 | bytes 7471616 | tf_op jit(solution)/shard_map/dot_general | solution.py:23
  175.4 35.8 %collective-permute-done.3 = bf16[256,2048]{0,1:T(8,128)(2,1)} collective-permute-done((bf16[256,2048]{0,1:T(8,128)(2,1)}, bf16[256,2048]{0,1:T(8,128)(2,1)}, u32[]{:S(2)}, u32[]{:S(2)}) %collective-permute-start.3) | collective-permute-done | bytes 1048608 | tf_op jit(solution)/shard_map/ppermute | solution.py:10
  211.2 1.9 collective-permute-start.5
  213.1 4.9 %convolution_add_fusion.2 = f32[256,2048]{1,0:T(8,128)} fusion(f32[256,2048]{1,0:T(8,128)} %convolution_add_fusion.3, bf16[256,2048]{0,1:T(8,128)(2,1)} %collective-permute-done.1, bf16[2048,256]{1,0:T(8,128)(2,1)S(1)} %convolution_convert_fusion, bf16[256,7,256]{2,0,1:T(8,128)(2,1)} %param.8, pred[]{:T(512)} %bitcast.7), kind=kOutput, calls=%fused_computation.6 | convolution fusion | flops 537722880 | bytes 7471616 | tf_op jit(solution)/shard_map/dot_general | solution.py:23
  218.1 0.0 collective-permute-done.2
  218.1 3.9 %collective-permute-start.4 = (bf16[256,2048]{0,1:T(8,128)(2,1)}, bf16[256,2048]{0,1:T(8,128)(2,1)}, u32[]{:S(2)}, u32[]{:S(2)}) collective-permute-start(bf16[256,2048]{0,1:T(8,128)(2,1)} %collective-permute-done.2), channel_id=1, source_target_pairs={{0,15},{1,0},{2,1},{3,2},{4,3},{5,4},{6,5},{7,6},{8,7},{9,8},{10,9... | collective-permute-start | bytes 3145736 | tf_op jit(solution)/shard_map/ppermute | solution.py:10
  222.0 2.9 %fusion.25 = f32[256,2048]{1,0:T(8,128)S(1)} fusion(bf16[256,2048]{0,1:T(8,128)(2,1)} %collective-permute-done.3, bf16[2048,256]{1,0:T(8,128)(2,1)S(1)} %convolution_convert_fusion, bf16[256,7,256]{2,0,1:T(8,128)(2,1)} %param.8, pred[]{:T(512)} %bitcast.11), kind=kOutput, calls=%fused_computation.39 | convolution fusion | flops 537198592 | bytes 5374464 | tf_op jit(solution)/shard_map/dot_general | solution.py:23
  224.9 4.9 %fusion.1 = f32[256,2048]{1,0:T(8,128)} fusion(f32[256,2048]{1,0:T(8,128)S(1)} %fusion.25, f32[256,2048]{1,0:T(8,128)} %convolution_add_fusion.2, bf16[256,2048]{0,1:T(8,128)(2,1)} %collective-permute-done.2, bf16[2048,256]{1,0:T(8,128)(2,1)S(1)} %convolution_convert_fusion, bf16[256,7,256]{2,0,1:T(8,128)(2,1)} %param.8, pred[]{:T(512)} %bitcast.11), kind=kOutput, calls=%fused_computation.5 | convolution fusion | flops 538247168 | bytes 9568768 | tf_op jit(solution)/shard_map/dot_general | solution.py:23
  229.8 9.6 %collective-permute-done.5 = bf16[256,2048]{0,1:T(8,128)(2,1)} collective-permute-done((bf16[256,2048]{0,1:T(8,128)(2,1)}, bf16[256,2048]{0,1:T(8,128)(2,1)}, u32[]{:S(2)}, u32[]{:S(2)}) %collective-permute-start.5) | collective-permute-done | bytes 1048608 | tf_op jit(solution)/shard_map/ppermute | solution.py:10
  239.4 0.0 copy-start.1
  239.4 4.4 %fusion.24 = f32[256,2048]{1,0:T(8,128)} fusion(bf16[256,2048]{0,1:T(8,128)(2,1)} %collective-permute-done.5, bf16[2048,256]{1,0:T(8,128)(2,1)S(1)} %convolution_convert_fusion, bf16[256,7,256]{2,0,1:T(8,128)(2,1)} %param.8, pred[]{:T(512)} %bitcast.14), kind=kOutput, calls=%fused_computation.38 | convolution fusion | flops 537198592 | bytes 5374464 | tf_op jit(solution)/shard_map/dot_general | solution.py:23
  243.9 0.0 collective-permute-done.4
  243.9 0.0 copy-done.1
  243.9 4.6 %fusion.2 = bf16[256,2048]{1,0:T(8,128)(2,1)} fusion(f32[256,2048]{1,0:T(8,128)} %fusion.24, f32[256,2048]{1,0:T(8,128)S(1)} %copy-done.1, bf16[256,2048]{0,1:T(8,128)(2,1)} %collective-permute-done.4, bf16[2048,256]{1,0:T(8,128)(2,1)S(1)} %convolution_convert_fusion, bf16[256,7,256]{2,0,1:T(8,128)(2,1)} %param.8, pred[]{:T(512)} %bitcast.14), kind=kOutput, calls=%fused_computation.8 | convolution fusion | flops 538771456 | bytes 8520192 | tf_op jit(solution)/shard_map/dot_general | solution.py:23
  (8 shorter events, 0.1 us)
Async XLA Ops:
  6.5 106.4 %copy-start = (bf16[256,256]{1,0:T(8,128)(2,1)S(1)}, bf16[256,256]{1,0:T(8,128)(2,1)}, u32[]{:S(2)}) copy-start(bf16[256,256]{1,0:T(8,128)(2,1)} %param.7) | copy-start | bytes 393220
  11.8 21.9 %all-to-all-start = ((bf16[32,2,8,128]{3,2,1,0:T(8,128)(2,1)}), bf16[32,2,8,128]{3,2,1,0:T(8,128)(2,1)S(1)}, u32[]{:S(2)}, u32[]{:S(2)}) async-start(bf16[32,2,8,128]{3,2,1,0:T(8,128)(2,1)} %select_select_fusion), calls=%async_computation | async-start | bytes 262144 | tf_op jit(solution)/shard_map/all_to_all | solution.py:49
  24.4 88.6 %all-gather.2.cloned.1.call-start = ((), (), s32[]{:S(2)}) async-start(), calls=%async_computation.1 | async-start | bytes 1114112 | tf_op jit(solution)/shard_map/all_gather | solution.py:59
  114.7 47.7 %collective-permute-start.1 = (bf16[256,2048]{0,1:T(8,128)(2,1)S(1)}, bf16[256,2048]{0,1:T(8,128)(2,1)}, u32[]{:S(2)}, u32[]{:S(2)}) collective-permute-start(bf16[256,2048]{0,1:T(8,128)(2,1)S(1)} %bitcast.84), channel_id=1, source_target_pairs={{0,1},{1,2},{2,3},{3,4},{4,5},{5,6},{6,7},{7,8},{8,9},{9,10},{10,1... | collective-permute-start | bytes 3145736 | tf_op jit(solution)/shard_map/ppermute | solution.py:10
  116.6 48.3 %collective-permute-start = (bf16[256,2048]{0,1:T(8,128)(2,1)S(1)}, bf16[256,2048]{0,1:T(8,128)(2,1)}, u32[]{:S(2)}, u32[]{:S(2)}) collective-permute-start(bf16[256,2048]{0,1:T(8,128)(2,1)S(1)} %bitcast.85), channel_id=1, source_target_pairs={{0,15},{1,0},{2,1},{3,2},{4,3},{5,4},{6,5},{7,6},{8,7},{9,8},{10,9... | collective-permute-start | bytes 3145736 | tf_op jit(solution)/shard_map/ppermute | solution.py:10
  162.3 48.9 %collective-permute-start.3 = (bf16[256,2048]{0,1:T(8,128)(2,1)}, bf16[256,2048]{0,1:T(8,128)(2,1)}, u32[]{:S(2)}, u32[]{:S(2)}) collective-permute-start(bf16[256,2048]{0,1:T(8,128)(2,1)} %collective-permute-done.1), channel_id=1, source_target_pairs={{0,1},{1,2},{2,3},{3,4},{4,5},{5,6},{6,7},{7,8},{8,9},{9,10},{10,1... | collective-permute-start | bytes 3145736 | tf_op jit(solution)/shard_map/ppermute | solution.py:10
  164.9 53.2 %collective-permute-start.2 = (bf16[256,2048]{0,1:T(8,128)(2,1)}, bf16[256,2048]{0,1:T(8,128)(2,1)}, u32[]{:S(2)}, u32[]{:S(2)}) collective-permute-start(bf16[256,2048]{0,1:T(8,128)(2,1)} %collective-permute-done), channel_id=1, source_target_pairs={{0,15},{1,0},{2,1},{3,2},{4,3},{5,4},{6,5},{7,6},{8,7},{9,8},{10,9... | collective-permute-start | bytes 3145736 | tf_op jit(solution)/shard_map/ppermute | solution.py:10
  211.2 28.2 %collective-permute-start.5 = (bf16[256,2048]{0,1:T(8,128)(2,1)}, bf16[256,2048]{0,1:T(8,128)(2,1)}, u32[]{:S(2)}, u32[]{:S(2)}) collective-permute-start(bf16[256,2048]{0,1:T(8,128)(2,1)} %collective-permute-done.3), channel_id=1, source_target_pairs={{0,1},{1,2},{2,3},{3,4},{4,5},{5,6},{6,7},{7,8},{8,9},{9,10},{10,1... | collective-permute-start | bytes 3145736 | tf_op jit(solution)/shard_map/ppermute | solution.py:10
  218.1 25.8 %collective-permute-start.4 = (bf16[256,2048]{0,1:T(8,128)(2,1)}, bf16[256,2048]{0,1:T(8,128)(2,1)}, u32[]{:S(2)}, u32[]{:S(2)}) collective-permute-start(bf16[256,2048]{0,1:T(8,128)(2,1)} %collective-permute-done.2), channel_id=1, source_target_pairs={{0,15},{1,0},{2,1},{3,2},{4,3},{5,4},{6,5},{7,6},{8,7},{9,8},{10,9... | collective-permute-start | bytes 3145736 | tf_op jit(solution)/shard_map/ppermute | solution.py:10
  239.4 4.4 %copy-start.1 = (f32[256,2048]{1,0:T(8,128)S(1)}, f32[256,2048]{1,0:T(8,128)}, u32[]{:S(2)}) copy-start(f32[256,2048]{1,0:T(8,128)} %fusion.1) | copy-start | bytes 6291460
Sparse Core Ops, SparseCore 0:
  35.3 77.6 all-gather.1
where the time goes:
time: 256 us; the launch traced here: 255 us
  waiting for transfers between devices  174 us (68%)
  starting transfers between devices  30.1 us (12%)
  matrix products  30.1 us (12%)
  between operations  14.2 us (6%)
  other arithmetic  4.15 us (2%)
  local copies, waits for them, and re-layouts  2.74 us (1%)
    ppermute x6, waiting for transfers between devices, passed_along(): return lax.ppermute(value, axis, pairs)  87.2 us
    all_gather x1, waiting for transfers between devices, on_device(): lax.all_gather(needed, 'blk', axis=1, tiled=True)  77.8 us
    dot_general x7, matrix products, block_term(): return jnp.dot(masked_tile, source, preferred_element_type=jnp.float32)  28.4 us
    ppermute x6, starting transfers between devices, passed_along(): return lax.ppermute(value, axis, pairs)  17.5 us
    all_to_all x1, starting transfers between devices, on_device(): lax.all_to_all(outgoing, 'cluster', split_axis=0, concat_axis=0, tiled=True)  12.6 us
    all_to_all x1, waiting for transfers between devices, on_device(): lax.all_to_all(outgoing, 'cluster', split_axis=0, concat_axis=0, tiled=True)  9.07 us
  transfers between devices with their start and end apart: 8, of which 5 were waited for; matrix products, arithmetic and copies ran while one was open for 9% of the time, Pallas kernels for 0%

commit v1 on v0

v1 whole, which is shorter than its diff:
```python
import jax
import jax.numpy as jnp
from jax import lax
from jax.experimental import pallas as pl
from jax.experimental.pallas import tpu as pltpu
from jax.sharding import PartitionSpec as P

MESH = pl.DeviceIdType.MESH
F32 = jnp.float32
BF16 = jnp.bfloat16

YP, YM, ZZ = 0, 1, 2

PART, UP, DOWN, PART_UP, PART_DOWN, PART_DOWN2 = range(6)
SLOT_OFFSET = {PART: 1, UP: 2, DOWN: -2, PART_UP: 3, PART_DOWN: -1, PART_DOWN2: -3}

GATHER = [
    (ZZ, 0, 0, 0), (YP, 0, 0, 0), (YM, 0, 0, 0),
    (ZZ, 0, 0, 1), (YP, 0, 0, 1), (YM, 0, 0, 1),
    "basis",
    (YP, 0, -1, 0), (YM, 0, 1, 0), (ZZ, 0, -1, 0), (ZZ, 0, 1, 0),
    (YP, 0, -1, 1), (YM, 0, 1, 1), (ZZ, 0, -1, 1), (ZZ, 0, 1, 1),
    "fold0",
    (YP, 0, -2, 0), (YM, 0, 2, 0),
    (YP, 1, -1, 0), (YM, 1, 1, 0),
    (YP, 0, -2, 1), (YM, 0, 2, 1),
    (YP, 1, -1, 1), (YM, 1, 1, 1),
    "basis2",
    "fold1",
    (YP, 0, -3, 0), (YM, 0, 3, 1), (ZZ, 0, -3, 1), (ZZ, 0, 3, 0),
    (YP, 1, -2, 0), (YM, 1, 2, 1),
    "fold2",
    (ZZ, 0, 4, 0), (ZZ, 0, 4, 1),
    "fold3",
]
SENDS = [s for s in GATHER if not isinstance(s, str)]


def arrivals():
    count = {YP: 0, YM: 0, ZZ: 0}
    index, came = {}, {}
    for link, plane, dist, half in SENDS:
        k = count[link]
        count[link] += 1
        index[(link, plane, dist, half)] = k
        if link == ZZ:
            seen = (1 - plane, dist, half)
        else:
            step = -1 if link == YP else 1
            seen = (plane, dist + step, half)
        if abs(seen[1]) == 4:
            seen = (seen[0], 4, seen[2])
        assert seen not in came and seen != (0, 0, 0)
        came[seen] = (link, k)
    return index, came


INDEX, CAME = arrivals()


def gather_kernel(
    n_y, n_clust, coeff_ref, inter_ref, basis_ref, coul_hbm, reach_ref,
    n_out, w_out,
    coul_v, coul_f, coul_t, out_buf, in_buf, n_buf, b_buf, g_ref,
    coul_sem, nout_sem, a2a_send, a2a_recv, b_send, b_recv, ag_send, ag_recv,
):
    c = lax.axis_index("cluster")
    b = lax.axis_index("blk")
    y, z = b // 2, b % 2
    sign = 1 - 2 * z
    rows = basis_ref.shape[0]
    stops = coul_v.shape[1]
    half_stops = (stops - 1) // 2

    def at(yy, zz):
        return lax.rem(yy + 2 * n_y, n_y) * 2 + zz

    link_to = {YP: at(y + 1, z), YM: at(y - 1, z), ZZ: at(y, 1 - z)}

    coul_copy = pltpu.make_async_copy(coul_hbm, coul_v, coul_sem)
    coul_copy.start()

    barrier = pltpu.get_barrier_semaphore()

    def greet(i, _):
        pl.semaphore_signal(
            barrier, inc=1, device_id=(lax.rem(c + i, n_clust), b), device_id_type=MESH
        )
        return 0

    lax.fori_loop(1, n_clust, greet, 0)
    for link in (YP, YM, ZZ):
        pl.semaphore_signal(barrier, inc=1, device_id=(c, link_to[link]), device_id_type=MESH)

    inter = inter_ref[...]
    n_list = inter.shape[1]
    n_atoms = 32
    slot_rows = 16 * n_clust
    owner = inter // n_atoms
    local = inter - owner * n_atoms
    mine = (owner == c).astype(F32)
    tri = (
        lax.broadcasted_iota(jnp.int32, (n_list, n_list), 0)
        < lax.broadcasted_iota(jnp.int32, (n_list, n_list), 1)
    ).astype(F32)
    rank = jnp.dot(mine, tri, preferred_element_type=F32)
    spread = (
        lax.broadcasted_iota(jnp.int32, (slot_rows, n_clust), 0) // 16
        == lax.broadcasted_iota(jnp.int32, (slot_rows, n_clust), 1)
    ).astype(F32)
    mine_e = jnp.dot(spread, mine, preferred_element_type=F32)
    rank_e = jnp.dot(spread, rank, preferred_element_type=F32)
    local_e = jnp.dot(spread, local.astype(F32), preferred_element_type=F32)
    row = lax.broadcasted_iota(jnp.int32, (slot_rows, 1), 0)
    slot = ((row // 8) % 2).astype(F32)
    func = (row % 8).astype(F32)
    take = mine_e * (rank_e == slot).astype(F32)
    filled = jnp.sum(take, axis=1, keepdims=True)
    source = jnp.sum(take * local_e, axis=1, keepdims=True) * 8 + func
    source = jnp.where(filled > 0.5, source, -1.0)
    pick = (
        lax.broadcasted_iota(jnp.int32, (slot_rows, rows), 1).astype(F32) == source
    ).astype(BF16)
    coeff = coeff_ref[...].astype(F32).reshape(rows, coeff_ref.shape[2]).astype(BF16)
    out_buf[...] = jnp.dot(pick, coeff, preferred_element_type=F32).astype(BF16)

    pl.semaphore_wait(barrier, n_clust - 1 + 3)

    def a2a(i):
        to = lax.rem(c + i, n_clust)
        return pltpu.make_async_remote_copy(
            src_ref=out_buf.at[pl.ds(pl.multiple_of(to * 16, 16), 16)],
            dst_ref=in_buf.at[pl.ds(pl.multiple_of(c * 16, 16), 16)],
            send_sem=a2a_send.at[i],
            recv_sem=a2a_recv.at[i],
            device_id=(to, b),
            device_id_type=MESH,
        )

    def a2a_start(i, _):
        a2a(i).start()
        return 0

    lax.fori_loop(1, n_clust, a2a_start, 0)

    up = at(y + sign, z)
    down = at(y - sign, z)
    across = link_to[ZZ]

    def basis_copy(src, slot_at, k, to):
        return pltpu.make_async_remote_copy(
            src_ref=basis_ref if src is None else b_buf.at[src],
            dst_ref=b_buf.at[slot_at],
            send_sem=b_send.at[k],
            recv_sem=b_recv.at[slot_at],
            device_id=(c, to),
            device_id_type=MESH,
        )

    basis_sends = [
        basis_copy(None, PART, 0, across),
        basis_copy(None, DOWN, 1, up),
        basis_copy(None, UP, 2, down),
        basis_copy(PART, PART_UP, 3, down),
        basis_copy(UP, PART_DOWN, 4, across),
        basis_copy(PART_DOWN, PART_DOWN2, 5, up),
    ]
    got_basis = set()

    def need_basis(slot_at):
        if slot_at not in got_basis:
            got_basis.add(slot_at)
            next(s for s, k in zip(basis_sends, (PART, DOWN, UP, PART_UP, PART_DOWN, PART_DOWN2)) if k == slot_at).wait_recv()

    for k in range(3):
        basis_sends[k].start()

    own_list = inter_ref[pl.ds(c, 1), :]
    own_owner = (own_list // n_atoms).astype(F32)
    entry = lax.broadcasted_iota(jnp.int32, (rows, n_list), 0) // 8
    column = lax.broadcasted_iota(jnp.int32, (rows, n_list), 1)
    own_row = jnp.broadcast_to(own_owner, (rows, n_list))
    owner_col = jnp.sum(jnp.where(entry == column, own_row, 0.0), axis=1, keepdims=True)
    own_rank = jnp.sum(
        jnp.where((own_row == owner_col) & (column < entry), 1.0, 0.0), axis=1, keepdims=True
    )
    func_col = (lax.broadcasted_iota(jnp.int32, (rows, 1), 0) % 8).astype(F32)
    place = owner_col * 16 + own_rank * 8 + func_col
    unpack = (
        lax.broadcasted_iota(jnp.int32, (rows, slot_rows), 1).astype(F32) == place
    ).astype(BF16)
    own_at = pl.ds(pl.multiple_of(c * 16, 16), 16)
    in_buf[own_at, :] = out_buf[own_at, :]

    coul_copy.wait()
    part = 32

    def widen(i, _):
        at_rows = pl.ds(pl.multiple_of(i * part, part), part)
        wide = coul_v[at_rows].astype(F32)
        for side in range(rows // 128):
            coul_f[side, at_rows, 0:stops, :] = wide[:, :, side * 128 : (side + 1) * 128]
        return 0

    lax.fori_loop(0, rows // part, widen, 0)

    def a2a_wait(i, _):
        a2a(i).wait_recv()
        return 0

    lax.fori_loop(1, n_clust, a2a_wait, 0)
    chunk = jnp.dot(unpack, in_buf[...], preferred_element_type=F32)
    n_buf[b] = chunk.astype(BF16)

    def chunk_at(plane, dist):
        return at(y + dist, z if plane == 0 else 1 - z)

    half = rows // 2

    def gather(link, plane, dist, h):
        k = INDEX[(link, plane, dist, h)]
        where = n_buf.at[chunk_at(plane, dist), pl.ds(h * half, half)]
        return pltpu.make_async_remote_copy(
            src_ref=where,
            dst_ref=where,
            send_sem=ag_send.at[link, k],
            recv_sem=ag_recv.at[link, k],
            device_id=(c, link_to[link]),
            device_id_type=MESH,
        )

    have = {(0, 0, 0), (0, 0, 1)}

    def need(plane, dist, h):
        if abs(dist) == 4:
            dist = 4
        if (plane, dist, h) not in have:
            have.add((plane, dist, h))
            link, k = CAME[(plane, dist, h)]
            where = n_buf.at[chunk_at(plane, dist), pl.ds(h * half, half)]
            pltpu.make_async_remote_copy(
                src_ref=where, dst_ref=where, send_sem=ag_send.at[link, k],
                recv_sem=ag_recv.at[link, k], device_id=(c, link_to[link]), device_id_type=MESH,
            ).wait_recv()

    out_copies = []

    def fold(dist, first=False):
        for plane in (0, 1):
            for h in (0, 1):
                need(plane, dist, h)
        pair = lax.rem(y + dist + 2 * n_y, n_y) * 2
        copy = pltpu.make_async_copy(
            n_buf.at[pl.ds(pair, 2)], n_out.at[pl.ds(pair, 2)], nout_sem.at[len(out_copies)]
        )
        copy.start()
        out_copies.append(copy)
        both = jnp.concatenate([n_buf[pair], n_buf[pair + 1]], axis=1)
        term = lax.dot_general(both, both, (((1,), (1,)), ((), ())), preferred_element_type=F32)
        g_ref[...] = term if first else g_ref[...] + term

    def turn():
        flat = coul_f.reshape(rows // 128, rows * 8, 128)
        reach = reach_ref[0]
        for o in range(stops):
            within = jnp.where(abs(o - half_stops) <= reach, F32(1.0), F32(0.0))
            for side in range(rows // 128):
                tile = flat[side, pl.ds(o, rows, stride=8), :]
                coul_t[o, :, side * 128 : (side + 1) * 128] = tile * within

    for item in GATHER:
        if item == "basis":
            need_basis(PART)
            basis_sends[3].start()
            need_basis(UP)
            basis_sends[4].start()
        elif item == "basis2":
            need_basis(PART_DOWN)
            basis_sends[5].start()
        elif item == "fold0":
            fold(0, True)
            turn()
        elif item == "fold1":
            fold(1)
            fold(-1)
        elif item == "fold2":
            fold(2)
            fold(-2)
        elif item == "fold3":
            for slot_at in SLOT_OFFSET:
                need_basis(slot_at)
            fold(3)
            fold(-3)
            fold(4)
        else:
            need(*item[1:])
            gather(*item).start()

    basis = basis_ref[...]
    scale = (n_out.shape[0] * n_out.shape[2]) ** -0.5
    g = g_ref[...]
    g_hi = g.astype(BF16)
    g_lo = (g - g_hi.astype(F32)).astype(BF16)
    h = jnp.dot(basis, g_hi, preferred_element_type=F32) + jnp.dot(
        basis, g_lo, preferred_element_type=F32
    )
    h = (h * scale).astype(BF16)
    w = None
    for slot_at, offset in [(None, 0)] + list(SLOT_OFFSET.items()):
        other = basis if slot_at is None else b_buf[slot_at]
        density = lax.dot_general(h, other, (((1,), (1,)), ((), ())), preferred_element_type=F32)
        tile = (density * coul_t[half_stops + sign * offset]).astype(BF16)
        term = jnp.dot(tile, other, preferred_element_type=F32)
        w = term if w is None else w + term
    w_out[...] = w.astype(BF16)

    def a2a_sent(i, _):
        a2a(i).wait_send()
        return 0

    lax.fori_loop(1, n_clust, a2a_sent, 0)
    for copy in basis_sends:
        copy.wait_send()
    for item in SENDS:
        gather(*item).wait_send()
    for copy in out_copies:
        copy.wait()


def apply_kernel(w_ref, n_ref, out_ref):
    w = w_ref[...]
    for j in range(n_ref.shape[0] // 2):
        both = jnp.concatenate([n_ref[2 * j], n_ref[2 * j + 1]], axis=1)
        width = both.shape[1]
        out_ref[:, j * width : (j + 1) * width] = jnp.dot(
            w, both, preferred_element_type=F32
        ).astype(BF16)


def solution(mesh):
    n_clust, n_blk = mesh.shape["cluster"], mesh.shape["blk"]

    def on_device(coeff, intersection, basis_vals, coulomb, reach):
        rows, funcs = basis_vals.shape
        columns = coeff.shape[2]
        stops = coulomb.shape[1]
        vmem = pl.BlockSpec(memory_space=pltpu.VMEM)
        anyw = pl.BlockSpec(memory_space=pl.ANY)
        per_link = 10

        def body(*refs):
            gather_kernel(n_blk // 2, n_clust, *refs)

        needed, w = pl.pallas_call(
            body,
            out_shape=(
                jax.ShapeDtypeStruct((n_blk, funcs, columns), BF16),
                jax.ShapeDtypeStruct((rows, funcs), BF16),
            ),
            in_specs=[vmem, vmem, vmem, anyw, pl.BlockSpec(memory_space=pltpu.SMEM)],
            out_specs=(anyw, vmem),
            scratch_shapes=[
                pltpu.VMEM((rows, stops, rows), BF16),
                pltpu.VMEM((rows // 128, rows, 8, 128), F32),
                pltpu.VMEM((stops, rows, rows), F32),
                pltpu.VMEM((16 * n_clust, columns), BF16),
                pltpu.VMEM((16 * n_clust, columns), BF16),
                pltpu.VMEM((n_blk, funcs, columns), BF16),
                pltpu.VMEM((6, rows, funcs), BF16),
                pltpu.VMEM((funcs, funcs), F32),
                pltpu.SemaphoreType.DMA,
                pltpu.SemaphoreType.DMA((8,)),
                pltpu.SemaphoreType.DMA((n_clust,)),
                pltpu.SemaphoreType.DMA((n_clust,)),
                pltpu.SemaphoreType.DMA((6,)),
                pltpu.SemaphoreType.DMA((6,)),
                pltpu.SemaphoreType.DMA((3, per_link)),
                pltpu.SemaphoreType.DMA((3, per_link)),
            ],
            compiler_params=pltpu.CompilerParams(
                collective_id=0, has_side_effects=True, vmem_limit_bytes=48 * 2**20
            ),
            name="gather",
        )(coeff, intersection, basis_vals, coulomb, reach)

        group = 4
        return pl.pallas_call(
            apply_kernel,
            out_shape=jax.ShapeDtypeStruct((rows, n_blk * columns), BF16),
            grid=(n_blk // group,),
            in_specs=[
                pl.BlockSpec((rows, funcs), lambda i: (0, 0)),
                pl.BlockSpec((group, funcs, columns), lambda i: (i, 0, 0)),
            ],
            out_specs=pl.BlockSpec((rows, group * columns), lambda i: (0, i)),
            compiler_params=pltpu.CompilerParams(vmem_limit_bytes=16 * 2**20),
            name="apply",
        )(w, needed)

    return jax.shard_map(
        on_device,
        mesh=mesh,
        in_specs=(
            P("cluster", None, "blk"),
            P(),
            P(("cluster", "blk"), None),
            P(("cluster", "blk"), None, None),
            P(("cluster", "blk")),
        ),
        out_specs=P(("cluster", "blk"), None),
        check_vma=False,
    )
```

time: 256 us -> 46.8 us (0.18)
  the two profiles are of different devices: /device:TPU:114 before, /device:TPU:16 now
where the time goes in v1:
time: 46.8 us; the launch traced here: 46.7 us
  Pallas kernels  44.2 us (94%)
  local copies, waits for them, and re-layouts  1.75 us (4%)
  between operations  0.71 us (2%)
    pallas_call x1, Pallas kernels, on_device(): pl.pallas_call(body, out_shape=(jax.ShapeDtypeStruct((n_blk, funcs, colum...  42.1 us
    pallas_call x1, Pallas kernels, on_device(): pl.pallas_call(apply_kernel, out_shape=jax.ShapeDtypeStruct((rows, n_blk...  2.14 us
    unnamed x7, local copies, waits for them, and re-layouts  1.75 us

profile of v1, /device:TPU:16, one launch (start us, length us, event | category | flops | bytes accessed | tf_op | source)
XLA Modules:
  0.0 46.7 jit_solution(1949700978545548404)
XLA Ops:
  0.7 0.0 copy-start
  0.7 0.0 copy-start.1
  0.7 0.0 copy-start.2
  0.7 1.7 %copy.6.refs_3_ = bf16[256,7,256]{2,1,0:T(8,128)(2,1)S(1)} copy(bf16[256,7,256]{2,0,1:T(8,128)(2,1)} %param.8) | data formatting | bytes 1835008 | tf_op args[3]
  2.4 0.0 copy-done
  2.4 0.0 copy-done.1
  2.4 0.0 copy-done.2
  2.5 42.1 %gather.1 = (bf16[16,256,128]{2,1,0:T(8,128)(2,1)S(1)}, bf16[256,256]{1,0:T(8,128)(2,1)S(1)}) custom-call(bf16[32,8,128]{2,1,0:T(8,128)(2,1)S(1)} %copy-done.1, s32[32,32]{1,0:T(8,128)S(1)} %copy-done.2, bf16[256,256]{1,0:T(8,128)(2,1)S(1)} %copy-done, bf16[256,7,256]{2,1,0:T(8,128)(2,1)S(1)} %copy.6.refs_3_, s32[1]{0:T(128)S(6)} %copy.7.refs_4_), custom_call_target="tpu_custom_call" | custom-call | tf_op jit(solution)/shard_map/gather/pallas_call | solution.py:354
  44.5 2.1 %apply.1 = bf16[256,2048]{1,0:T(8,128)(2,1)} custom-call(bf16[256,256]{1,0:T(8,128)(2,1)S(1)} %get-tuple-element.7.w_ref, bf16[16,256,128]{2,1,0:T(8,128)(2,1)S(1)} %get-tuple-element.8.n_ref), custom_call_target="tpu_custom_call" | custom-call | tf_op jit(solution)/shard_map/apply/pallas_call | solution.py:387
Async XLA Ops:
  0.7 1.8 %copy-start = (bf16[256,256]{1,0:T(8,128)(2,1)S(1)}, bf16[256,256]{1,0:T(8,128)(2,1)}, u32[]{:S(2)}) copy-start(bf16[256,256]{1,0:T(8,128)(2,1)} %refs_2_.1) | copy-start | bytes 393220
  0.7 1.8 %copy-start.1 = (bf16[32,8,128]{2,1,0:T(8,128)(2,1)S(1)}, bf16[32,8,128]{2,1,0:T(8,128)(2,1)}, u32[]{:S(2)}) copy-start(bf16[32,8,128]{2,1,0:T(8,128)(2,1)} %refs_0_.1) | copy-start | bytes 196612
  0.7 1.8 %copy-start.2 = (s32[32,32]{1,0:T(8,128)S(1)}, s32[32,32]{1,0:T(8,128)}, u32[]{:S(2)}) copy-start(s32[32,32]{1,0:T(8,128)} %refs_1_.1) | copy-start | bytes 12292

commit v2 on v0

v2 whole, which is shorter than its diff:
```python
import jax
import jax.numpy as jnp
from jax import lax
from jax.experimental import pallas as pl
from jax.experimental.pallas import tpu as pltpu
from jax.sharding import PartitionSpec as P

MESH = pl.DeviceIdType.MESH
F32 = jnp.float32
BF16 = jnp.bfloat16

PART, UP, DOWN, PART_UP, PART_DOWN, PART_DOWN2 = range(6)
SLOT_OFFSET = {PART: 1, UP: 2, DOWN: -2, PART_UP: 3, PART_DOWN: -1, PART_DOWN2: -3}

PARTS = 4
FIRST = [
    (0, 1, 0, 0, 0, 4),
    (2, 0, 0, 0, 0, 4), (-2, 0, 0, 0, 0, 4),
    (1, 0, 0, 0, 0, 4), (-1, 0, 0, 0, 0, 4),
]
THEN = [
    (1, 0, 1, 0, 0, 4), (-1, 0, 1, 0, 0, 4),
    ((0, 0), (1, 0)),
    (2, 0, 0, -2, 0, 2), (-2, 0, 0, 2, 2, 4),
    (1, 0, 0, -2, 0, 4), (-1, 0, 0, 2, 0, 4),
    (0, 1, 0, -2, 0, 4), (0, 1, 0, 2, 0, 4),
    "basis",
    ((0, 1), (0, -1)), ((0, 2), (0, -2)), ((1, 1), (1, -1)),
    (0, 1, 0, 4, 0, 2), (0, 1, 0, 4, 2, 4),
    (0, 1, 0, -3, 0, 4), (0, 1, 0, 3, 0, 4),
    ((0, 3), (0, -3)), ((1, 2), (1, -2)), ((0, 4), (1, 4)), ((1, 3), (1, -3)),
]
SENDS = FIRST + [s for s in THEN if len(s) == 6]


def wrapped(dist):
    return (dist + 3) % 8 - 3


def arrivals():
    came = {}
    for k, (up, across, plane, dist, first, end) in enumerate(SENDS):
        for part in range(first, end):
            key = ((plane + across) % 2, wrapped(dist - up), part)
            assert key not in came and key[:2] != (0, 0)
            came[key] = k
    assert len(came) == 15 * PARTS
    return came


CAME = arrivals()


def at(yy, zz, n_y):
    return lax.rem(yy + 2 * n_y, n_y) * 2 + zz


def exchange(n_y, basis_hbm, blocks, send_sem, recv_sem):
    c = lax.axis_index("cluster")
    b = lax.axis_index("blk")
    y, z = b // 2, b % 2
    sign = 1 - 2 * z
    up, down, across = at(y + sign, z, n_y), at(y - sign, z, n_y), at(y, 1 - z, n_y)

    def copy(src, slot_at, to):
        return pltpu.make_async_remote_copy(
            src_ref=basis_hbm if src is None else blocks.at[src],
            dst_ref=blocks.at[slot_at],
            send_sem=send_sem.at[slot_at],
            recv_sem=recv_sem.at[slot_at],
            device_id=(c, to),
            device_id_type=MESH,
        )

    copies = [
        copy(None, PART, across),
        copy(None, UP, down),
        copy(None, DOWN, up),
        copy(PART, PART_UP, down),
        copy(UP, PART_DOWN, across),
        copy(PART_DOWN, PART_DOWN2, up),
    ]

    def begin():
        for k in (PART, UP, DOWN):
            copies[k].start()

    def relay():
        copies[PART].wait_recv()
        copies[PART_UP].start()
        copies[UP].wait_recv()
        copies[PART_DOWN].start()

    def relay_last():
        copies[PART_DOWN].wait_recv()
        copies[PART_DOWN2].start()

    def finish():
        for k in (DOWN, PART_UP, PART_DOWN2):
            copies[k].wait_recv()
        for k in range(6):
            copies[k].wait_send()

    return begin, relay, relay_last, finish


def gather_kernel(
    n_y, n_clust, coeff_hbm, inter_hbm, basis_hbm, coul_hbm, reach_ref,
    n_buf, w_out,
    coeff_ref, inter_ref, basis_ref, coul_v, coeff_f, out_f, out_buf, in_buf, blocks, g_ref,
    load_sem, a2a_send, a2a_recv, b_send, b_recv, ag_send, ag_recv,
):
    c = lax.axis_index("cluster")
    b = lax.axis_index("blk")
    y, z = b // 2, b % 2
    sign = 1 - 2 * z
    rows = basis_ref.shape[0]
    stops = coul_v.shape[0]
    half_stops = (stops - 1) // 2

    inter_load, coeff_load, basis_load, coul_load = [
        pltpu.make_async_copy(src, dst, load_sem.at[k])
        for k, (src, dst) in enumerate(
            (
                (inter_hbm, inter_ref),
                (coeff_hbm, coeff_ref),
                (basis_hbm, basis_ref),
                (coul_hbm, coul_v),
            )
        )
    ]
    inter_load.start()
    coeff_load.start()

    barrier = pltpu.get_barrier_semaphore()

    def greet(to, _):
        @pl.when(to != c)
        def _():
            pl.semaphore_signal(barrier, inc=1, device_id=(to, b), device_id_type=MESH)

        return 0

    lax.fori_loop(0, n_clust, greet, 0)
    greeted = [(y + d, z) for d in (1, -1, 2, -2)] + [(y, 1 - z)]
    for yy, zz in greeted:
        pl.semaphore_signal(
            barrier, inc=1, device_id=(c, at(yy, zz, n_y)), device_id_type=MESH
        )

    inter_load.wait()
    inter = inter_ref[...]
    n_list = inter.shape[1]
    n_atoms, funcs, columns = coeff_ref.shape
    slot_rows = 2 * funcs * n_clust
    owner = inter // n_atoms
    key = lax.broadcasted_iota(jnp.int32, inter.shape, 1) * n_atoms + (inter - owner * n_atoms)
    key = key.astype(F32)
    top = F32(n_list * n_atoms)
    low = jnp.min(jnp.where(owner == c, key, top), axis=1, keepdims=True)
    high = jnp.max(jnp.where(owner == c, key, -1.0), axis=1, keepdims=True)
    low_at = jnp.where(low < top, low.astype(jnp.int32) % n_atoms, -1)
    high_at = jnp.where(high > low, high.astype(jnp.int32) % n_atoms, -1)
    atom = lax.broadcasted_iota(jnp.int32, (n_clust, n_atoms), 1)
    pick = jnp.concatenate([atom == low_at, atom == high_at], axis=0).astype(F32).astype(BF16)
    coeff_load.wait()
    coeff_f[...] = coeff_ref[...].astype(F32).reshape(n_atoms * funcs, columns)
    by_atom = jnp.concatenate(
        [coeff_f[pl.ds(m, n_atoms, stride=funcs), :].astype(BF16) for m in range(funcs)], axis=1
    )
    packed = jnp.dot(pick, by_atom, preferred_element_type=F32)
    for s in range(2):
        for m in range(funcs):
            out_f[pl.ds(s * funcs + m, n_clust, stride=2 * funcs), :] = packed[
                s * n_clust : (s + 1) * n_clust, m * columns : (m + 1) * columns
            ]
    out_buf[...] = out_f[...].astype(BF16)

    pl.semaphore_wait(barrier, n_clust - 1 + len(greeted))

    def a2a(to, source):
        return pltpu.make_async_remote_copy(
            src_ref=out_buf.at[pl.ds(pl.multiple_of(to * 16, 16), 16)],
            dst_ref=in_buf.at[pl.ds(pl.multiple_of(source * 16, 16), 16)],
            send_sem=a2a_send.at[to],
            recv_sem=a2a_recv.at[source],
            device_id=(to, b),
            device_id_type=MESH,
        )

    def a2a_start(to, _):
        @pl.when(to != c)
        def _():
            a2a(to, c).start()

        return 0

    lax.fori_loop(0, n_clust, a2a_start, 0)
    begin_basis, relay_basis, relay_basis_last, finish_basis = exchange(
        n_y, basis_hbm, blocks, b_send, b_recv
    )
    begin_basis()
    basis_load.start()
    coul_load.start()

    own_list = inter_ref[pl.ds(c, 1), :]
    own_owner = (own_list // n_atoms).astype(F32)
    entry = lax.broadcasted_iota(jnp.int32, (rows, n_list), 0) // funcs
    column = lax.broadcasted_iota(jnp.int32, (rows, n_list), 1)
    own_row = jnp.broadcast_to(own_owner, (rows, n_list))
    owner_col = jnp.sum(jnp.where(entry == column, own_row, 0.0), axis=1, keepdims=True)
    own_rank = jnp.sum(
        jnp.where((own_row == owner_col) & (column < entry), 1.0, 0.0), axis=1, keepdims=True
    )
    func_col = (lax.broadcasted_iota(jnp.int32, (rows, 1), 0) % funcs).astype(F32)
    place = owner_col * (2 * funcs) + own_rank * funcs + func_col
    unpack = (
        lax.broadcasted_iota(jnp.int32, (rows, slot_rows), 1).astype(F32) == place
    ).astype(BF16)
    own_at = pl.ds(pl.multiple_of(c * 16, 16), 16)
    in_buf[own_at, :] = out_buf[own_at, :]

    def a2a_wait(source, _):
        @pl.when(source != c)
        def _():
            a2a(c, source).wait_recv()

        return 0

    lax.fori_loop(0, n_clust, a2a_wait, 0)
    chunk = jnp.dot(unpack, in_buf[...], preferred_element_type=F32)
    n_buf[b] = chunk.astype(BF16)

    def chunk_at(plane, dist):
        return at(y + dist, z if plane == 0 else 1 - z, n_y)

    part_rows = rows // PARTS

    def send(k):
        rise, across, plane, dist, first, end = SENDS[k]
        where = n_buf.at[
            chunk_at(plane, dist), pl.ds(first * part_rows, (end - first) * part_rows)
        ]
        return pltpu.make_async_remote_copy(
            src_ref=where,
            dst_ref=where,
            send_sem=ag_send.at[k],
            recv_sem=ag_recv.at[k],
            device_id=(c, at(y + rise, 1 - z if across else z, n_y)),
            device_id_type=MESH,
        )

    have = set()

    def need(plane, dist, first=0, end=PARTS):
        if (plane, dist) == (0, 0):
            return
        for part in range(first, end):
            k = CAME[(plane, wrapped(dist), part)]
            if k not in have:
                have.add(k)
                send(k).wait_recv()

    for k in range(len(FIRST)):
        send(k).start()
    relay_basis()
    k = len(FIRST)
    folded = False
    for item in THEN:
        if item == "basis":
            relay_basis_last()
        elif len(item) == 6:
            need(*item[2:])
            send(k).start()
            k += 1
        else:
            for chunk_of in item:
                need(*chunk_of)
            both = jnp.concatenate([n_buf[chunk_at(*chunk_of)] for chunk_of in item], axis=1)
            term = lax.dot_general(both, both, (((1,), (1,)), ((), ())), preferred_element_type=F32)
            g_ref[...] = g_ref[...] + term if folded else term
            folded = True
    finish_basis()

    basis_load.wait()
    basis = basis_ref[...]
    scale = (n_buf.shape[0] * n_buf.shape[2]) ** -0.5
    g = g_ref[...]
    g_hi = g.astype(BF16)
    g_lo = (g - g_hi.astype(F32)).astype(BF16)
    h = jnp.dot(basis, g_hi, preferred_element_type=F32) + jnp.dot(
        basis, g_lo, preferred_element_type=F32
    )
    h = (h * scale).astype(BF16)
    coul_load.wait()
    reach = reach_ref[0]
    w = None
    for slot_at, offset in [(None, 0)] + list(SLOT_OFFSET.items()):
        other = basis if slot_at is None else blocks[slot_at]
        density = lax.dot_general(h, other, (((1,), (1,)), ((), ())), preferred_element_type=F32)
        within = jnp.where(abs(offset) <= reach, F32(1.0), F32(0.0))
        coul = coul_v[half_stops + sign * offset].astype(F32) * within
        tile = (density * coul).astype(BF16)
        term = jnp.dot(tile, other, preferred_element_type=F32)
        w = term if w is None else w + term
    w_out[...] = w.astype(BF16)

    def a2a_sent(to, _):
        @pl.when(to != c)
        def _():
            a2a(to, c).wait_send()

        return 0

    lax.fori_loop(0, n_clust, a2a_sent, 0)
    for k in range(len(SENDS)):
        send(k).wait_send()


def apply_kernel(w_ref, n_ref, out_hbm, out_v, sem):
    w = w_ref[...]
    width = 2 * n_ref.shape[2]
    copies = []
    for j in range(n_ref.shape[0] // 2):
        both = jnp.concatenate([n_ref[2 * j], n_ref[2 * j + 1]], axis=1)
        where = slice(j * width, (j + 1) * width)
        out_v[:, where] = jnp.dot(w, both, preferred_element_type=F32).astype(BF16)
        copy = pltpu.make_async_copy(out_v.at[:, where], out_hbm.at[:, where], sem.at[j])
        copy.start()
        copies.append(copy)
    for copy in copies:
        copy.wait()


def solution(mesh):
    n_clust, n_blk = mesh.shape["cluster"], mesh.shape["blk"]
    n_y = n_blk // 2

    def on_device(coeff, intersection, basis_vals, coulomb, reach):
        rows, funcs = basis_vals.shape
        columns = coeff.shape[2]
        stops = coulomb.shape[1]
        vmem = pl.BlockSpec(memory_space=pltpu.VMEM)
        hbm = pl.BlockSpec(memory_space=pltpu.HBM)

        def stay(x):
            return pltpu.with_memory_space_constraint(x, pltpu.HBM)

        basis_vals = stay(basis_vals)

        def gather(*refs):
            gather_kernel(n_y, n_clust, *refs)

        needed, w = pl.pallas_call(
            gather,
            out_shape=(
                jax.ShapeDtypeStruct((n_blk, funcs, columns), BF16),
                jax.ShapeDtypeStruct((rows, funcs), BF16),
            ),
            in_specs=[hbm, hbm, hbm, hbm, pl.BlockSpec(memory_space=pltpu.SMEM)],
            out_specs=(vmem, vmem),
            scratch_shapes=[
                pltpu.VMEM(coeff.shape, BF16),
                pltpu.VMEM(intersection.shape, jnp.int32),
                pltpu.VMEM((rows, funcs), BF16),
                pltpu.VMEM((stops, rows, rows), BF16),
                pltpu.VMEM((coeff.shape[0] * coeff.shape[1], columns), F32),
                pltpu.VMEM((16 * n_clust, columns), F32),
                pltpu.VMEM((16 * n_clust, columns), BF16),
                pltpu.VMEM((16 * n_clust, columns), BF16),
                pltpu.VMEM((6, rows, funcs), BF16),
                pltpu.VMEM((funcs, funcs), F32),
                pltpu.SemaphoreType.DMA((4,)),
                pltpu.SemaphoreType.DMA((n_clust,)),
                pltpu.SemaphoreType.DMA((n_clust,)),
                pltpu.SemaphoreType.DMA((6,)),
                pltpu.SemaphoreType.DMA((6,)),
                pltpu.SemaphoreType.DMA((len(SENDS),)),
                pltpu.SemaphoreType.DMA((len(SENDS),)),
            ],
            compiler_params=pltpu.CompilerParams(
                collective_id=0, has_side_effects=True, vmem_limit_bytes=32 * 2**20
            ),
            name="gather",
        )(
            stay(coeff),
            stay(intersection),
            basis_vals,
            stay(jnp.swapaxes(coulomb, 0, 1)),
            reach,
        )

        return pl.pallas_call(
            apply_kernel,
            out_shape=jax.ShapeDtypeStruct((rows, n_blk * columns), BF16),
            in_specs=[vmem, vmem],
            out_specs=hbm,
            scratch_shapes=[
                pltpu.VMEM((rows, n_blk * columns), BF16),
                pltpu.SemaphoreType.DMA((n_blk // 2,)),
            ],
            compiler_params=pltpu.CompilerParams(vmem_limit_bytes=16 * 2**20),
            name="apply",
        )(w, needed)

    return jax.shard_map(
        on_device,
        mesh=mesh,
        in_specs=(
            P("cluster", None, "blk"),
            P(),
            P(("cluster", "blk"), None),
            P(("cluster", "blk"), None, None),
            P(("cluster", "blk")),
        ),
        out_specs=P(("cluster", "blk"), None),
        check_vma=False,
    )
```

time: 256 us -> 43.5 us (0.17)
  the two profiles are of different devices: /device:TPU:114 before, /device:TPU:4 now
where the time goes in v2:
time: 43.5 us; the launch traced here: 43.3 us
  Pallas kernels  42.7 us (98%)
  between operations  0.66 us (2%)
    pallas_call x1, Pallas kernels, on_device(): pl.pallas_call(gather, out_shape=(jax.ShapeDtypeStruct((n_blk, funcs, col...  41.4 us
    pallas_call x1, Pallas kernels, on_device(): pl.pallas_call(apply_kernel, out_shape=jax.ShapeDtypeStruct((rows, n_blk...  1.26 us

profile of v2, /device:TPU:4, one launch (start us, length us, event | category | flops | bytes accessed | tf_op | source)
XLA Modules:
  0.0 43.3 jit_solution(32660335007186643)
XLA Ops:
  0.7 41.4 %gather.1 = (bf16[16,256,128]{2,1,0:T(8,128)(2,1)S(1)}, bf16[256,256]{1,0:T(8,128)(2,1)S(1)}) custom-call(bf16[32,8,128]{2,1,0:T(8,128)(2,1)} %refs_0_.1, s32[32,32]{1,0:T(8,128)} %refs_1_.1, bf16[256,256]{1,0:T(8,128)(2,1)} %refs_2_.1, bf16[7,256,256]{2,1,0:T(8,128)(2,1)} %bitcast.1, s32[1]{0:T(128)S(6)} %copy.6.refs_4_), custom_call_target="tpu_custom_call" | custom-call | tf_op jit(solution)/shard_map/gather/pallas_call | solution.py:354
  42.1 1.3 %apply.1 = bf16[256,2048]{1,0:T(8,128)(2,1)} custom-call(bf16[256,256]{1,0:T(8,128)(2,1)S(1)} %get-tuple-element.7.w_ref, bf16[16,256,128]{2,1,0:T(8,128)(2,1)S(1)} %get-tuple-element.8.n_ref), custom_call_target="tpu_custom_call" | custom-call | tf_op jit(solution)/shard_map/apply/pallas_call | solution.py:393

commit v3 on v2

--- a/solution.py
+++ b/solution.py
@@ -12,24 +12,24 @@
 PART, UP, DOWN, PART_UP, PART_DOWN, PART_DOWN2 = range(6)
 SLOT_OFFSET = {PART: 1, UP: 2, DOWN: -2, PART_UP: 3, PART_DOWN: -1, PART_DOWN2: -3}
 
+GROUPS = 4
 PARTS = 4
 FIRST = [
-    (0, 1, 0, 0, 0, 4),
-    (2, 0, 0, 0, 0, 4), (-2, 0, 0, 0, 0, 4),
-    (1, 0, 0, 0, 0, 4), (-1, 0, 0, 0, 0, 4),
+    (-1, 0, 0, 0, 2, 4), (1, 0, 0, 0, 2, 4), (0, 1, 0, 0, 0, 2), (-1, 0, 0, 0, 0, 2), (1, 0, 0, 0, 0, 2),
+    (-3, 0, 0, 0, 0, 2), (3, 0, 0, 0, 0, 2), (0, 1, 0, 0, 2, 4),
 ]
 THEN = [
-    (1, 0, 1, 0, 0, 4), (-1, 0, 1, 0, 0, 4),
-    ((0, 0), (1, 0)),
-    (2, 0, 0, -2, 0, 2), (-2, 0, 0, 2, 2, 4),
-    (1, 0, 0, -2, 0, 4), (-1, 0, 0, 2, 0, 4),
-    (0, 1, 0, -2, 0, 4), (0, 1, 0, 2, 0, 4),
-    "basis",
-    ((0, 1), (0, -1)), ((0, 2), (0, -2)), ((1, 1), (1, -1)),
-    (0, 1, 0, 4, 0, 2), (0, 1, 0, 4, 2, 4),
-    (0, 1, 0, -3, 0, 4), (0, 1, 0, 3, 0, 4),
-    ((0, 3), (0, -3)), ((1, 2), (1, -2)), ((0, 4), (1, 4)), ((1, 3), (1, -3)),
+    (0, 1, 0, 1, 2, 4), (0, 1, 0, -1, 2, 4), (-2, 0, 0, 1, 2, 4), (2, 0, 0, -1, 2, 4),
+    (-1, 0, 0, 1, 2, 4), (1, 0, 0, -1, 2, 4), (0, 1, 0, 1, 0, 2), (0, 1, 0, -1, 0, 2),
+    (-1, 0, 0, 1, 0, 2), (1, 0, 0, -1, 0, 2),
+    ((0, 0), (1, 0)), ((0, 1), (0, -1)),
+    (0, 1, 0, 3, 0, 2), (0, 1, 0, -3, 0, 2), (-1, 0, 1, 1, 2, 4), (1, 0, 1, -1, 2, 4),
+    (0, 1, 0, 3, 2, 4), (0, 1, 0, -3, 2, 4), (-1, 1, 0, 3, 0, 2), (1, 1, 0, -3, 2, 4),
+    (1, 0, 0, -3, 0, 2), (-1, 0, 0, 3, 2, 4), (-1, 0, 1, 1, 0, 2), (1, 0, 1, -1, 0, 2),
+    ((0, 3), (0, -3)), ((1, 1), (1, -1)), ((0, 2), (0, -2)),
+    ((1, 2), (1, -2)), ((0, 4), (1, 4)), ((1, 3), (1, -3)),
 ]
+TARGETS = sorted({s[:2] for s in FIRST} | {s[:2] for s in THEN if len(s) == 6})
 SENDS = FIRST + [s for s in THEN if len(s) == 6]
 
 
@@ -134,6 +134,10 @@
 
     barrier = pltpu.get_barrier_semaphore()
 
+    group = n_clust // GROUPS
+    mine = c // group
+    first_mate, first_later = mine * group, (mine + 1) * group
+
     def greet(to, _):
         @pl.when(to != c)
         def _():
@@ -141,11 +145,13 @@
 
         return 0
 
-    lax.fori_loop(0, n_clust, greet, 0)
-    greeted = [(y + d, z) for d in (1, -1, 2, -2)] + [(y, 1 - z)]
-    for yy, zz in greeted:
+    lax.fori_loop(first_mate, n_clust, greet, 0)
+    for rise, across in TARGETS:
         pl.semaphore_signal(
-            barrier, inc=1, device_id=(c, at(yy, zz, n_y)), device_id_type=MESH
+            barrier,
+            inc=1,
+            device_id=(c, at(y + rise, 1 - z if across else z, n_y)),
+            device_id_type=MESH,
         )
 
     inter_load.wait()
@@ -176,7 +182,7 @@
             ]
     out_buf[...] = out_f[...].astype(BF16)
 
-    pl.semaphore_wait(barrier, n_clust - 1 + len(greeted))
+    pl.semaphore_wait(barrier, first_later - 1 + len(TARGETS))
 
     def a2a(to, source):
         return pltpu.make_async_remote_copy(
@@ -195,7 +201,7 @@
 
         return 0
 
-    lax.fori_loop(0, n_clust, a2a_start, 0)
+    lax.fori_loop(0, first_later, a2a_start, 0)
     begin_basis, relay_basis, relay_basis_last, finish_basis = exchange(
         n_y, basis_hbm, blocks, b_send, b_recv
     )
@@ -227,7 +233,24 @@
 
         return 0
 
-    lax.fori_loop(0, n_clust, a2a_wait, 0)
+    lax.fori_loop(first_mate, first_later, a2a_wait, 0)
+    relay_basis()
+
+    def answer(source, _):
+        a2a(c, source).wait_recv()
+        a2a(source, c).start()
+        return 0
+
+    for later in range(1, GROUPS):
+        if later == GROUPS // 2:
+            pl.when(mine < later)(relay_basis_last)
+
+        @pl.when(mine < later)
+        def _():
+            lax.fori_loop(later * group, (later + 1) * group, answer, 0)
+
+    pl.when(mine >= GROUPS // 2)(relay_basis_last)
+    lax.fori_loop(0, first_mate, a2a_wait, 0)
     chunk = jnp.dot(unpack, in_buf[...], preferred_element_type=F32)
     n_buf[b] = chunk.astype(BF16)
 
@@ -263,13 +286,10 @@
 
     for k in range(len(FIRST)):
         send(k).start()
-    relay_basis()
     k = len(FIRST)
     folded = False
     for item in THEN:
-        if item == "basis":
-            relay_basis_last()
-        elif len(item) == 6:
+        if len(item) == 6:
             need(*item[2:])
             send(k).start()
             k += 1

time: 43.5 us -> 41.1 us (0.945)
  the two profiles are of different devices: /device:TPU:4 before, /device:TPU:256 now
where the time goes in v3:
time: 41.1 us; the launch traced here: 40.9 us
  Pallas kernels  40.3 us (98%)
  between operations  0.66 us (2%)
    pallas_call x1, Pallas kernels, on_device(): pl.pallas_call(gather, out_shape=(jax.ShapeDtypeStruct((n_blk, funcs, col...  39 us
    pallas_call x1, Pallas kernels, on_device(): pl.pallas_call(apply_kernel, out_shape=jax.ShapeDtypeStruct((rows, n_blk...  1.26 us

profile of v3, /device:TPU:256, one launch (start us, length us, event | category | flops | bytes accessed | tf_op | source)
XLA Modules:
  0.0 40.9 jit_solution(3291922592966386861)
XLA Ops:
  0.7 39.0 %gather.1 = (bf16[16,256,128]{2,1,0:T(8,128)(2,1)S(1)}, bf16[256,256]{1,0:T(8,128)(2,1)S(1)}) custom-call(bf16[32,8,128]{2,1,0:T(8,128)(2,1)} %refs_0_.1, s32[32,32]{1,0:T(8,128)} %refs_1_.1, bf16[256,256]{1,0:T(8,128)(2,1)} %refs_2_.1, bf16[7,256,256]{2,1,0:T(8,128)(2,1)} %bitcast.1, s32[1]{0:T(128)S(6)} %copy.6.refs_4_), custom_call_target="tpu_custom_call" | custom-call | tf_op jit(solution)/shard_map/gather/pallas_call | solution.py:374
  39.6 1.3 %apply.1 = bf16[256,2048]{1,0:T(8,128)(2,1)} custom-call(bf16[256,256]{1,0:T(8,128)(2,1)S(1)} %get-tuple-element.7.w_ref, bf16[16,256,128]{2,1,0:T(8,128)(2,1)S(1)} %get-tuple-element.8.n_ref), custom_call_target="tpu_custom_call" | custom-call | tf_op jit(solution)/shard_map/apply/pallas_call | solution.py:413

commit v4 on v3

--- a/solution.py
+++ b/solution.py
@@ -13,23 +13,54 @@
 SLOT_OFFSET = {PART: 1, UP: 2, DOWN: -2, PART_UP: 3, PART_DOWN: -1, PART_DOWN2: -3}
 
 GROUPS = 4
+PIECES = 4
 PARTS = 4
 FIRST = [
-    (-1, 0, 0, 0, 2, 4), (1, 0, 0, 0, 2, 4), (0, 1, 0, 0, 0, 2), (-1, 0, 0, 0, 0, 2), (1, 0, 0, 0, 0, 2),
-    (-3, 0, 0, 0, 0, 2), (3, 0, 0, 0, 0, 2), (0, 1, 0, 0, 2, 4),
+    (-1, 0, 0, 0, 0, 2),
+    (1, 0, 0, 0, 0, 2),
+    (0, 1, 0, 0, 2, 4),
+    (-2, 0, 0, 0, 2, 4),
+    (2, 0, 0, 0, 2, 4),
+    (0, 1, 0, 0, 0, 2),
+    (-1, 0, 0, 0, 2, 4),
+    (1, 0, 0, 0, 2, 4),
 ]
 THEN = [
-    (0, 1, 0, 1, 2, 4), (0, 1, 0, -1, 2, 4), (-2, 0, 0, 1, 2, 4), (2, 0, 0, -1, 2, 4),
-    (-1, 0, 0, 1, 2, 4), (1, 0, 0, -1, 2, 4), (0, 1, 0, 1, 0, 2), (0, 1, 0, -1, 0, 2),
-    (-1, 0, 0, 1, 0, 2), (1, 0, 0, -1, 0, 2),
-    ((0, 0), (1, 0)), ((0, 1), (0, -1)),
-    (0, 1, 0, 3, 0, 2), (0, 1, 0, -3, 0, 2), (-1, 0, 1, 1, 2, 4), (1, 0, 1, -1, 2, 4),
-    (0, 1, 0, 3, 2, 4), (0, 1, 0, -3, 2, 4), (-1, 1, 0, 3, 0, 2), (1, 1, 0, -3, 2, 4),
-    (1, 0, 0, -3, 0, 2), (-1, 0, 0, 3, 2, 4), (-1, 0, 1, 1, 0, 2), (1, 0, 1, -1, 0, 2),
-    ((0, 3), (0, -3)), ((1, 1), (1, -1)), ((0, 2), (0, -2)),
-    ((1, 2), (1, -2)), ((0, 4), (1, 4)), ((1, 3), (1, -3)),
+    (0, 1, 0, 1, 0, 2),
+    (0, 1, 0, -1, 0, 2),
+    (-2, 0, 0, 1, 0, 2),
+    (2, 0, 0, -1, 0, 2),
+    (0, 1, 0, 2, 2, 4),
+    (0, 1, 0, -2, 2, 4),
+    (-1, 0, 0, 2, 2, 4),
+    (1, 0, 0, -2, 2, 4),
+    (-1, 0, 0, 1, 0, 2),
+    (1, 0, 0, -1, 0, 2),
+    (-1, 0, 1, 0, 2, 4),
+    (1, 0, 1, 0, 2, 4),
+    (-1, 0, 1, 1, 0, 2),
+    (1, 0, 1, -1, 0, 2),
+    (0, 1, 0, 3, 0, 2),
+    (0, 1, 0, -3, 0, 2),
+    (1, 1, 0, -3, 0, 2),
+    (-1, 1, 0, 3, 2, 4),
+    (-1, 0, 0, 3, 0, 2),
+    (1, 0, 0, -3, 2, 4),
+    (-1, 0, 1, 2, 2, 4),
+    (1, 0, 1, -2, 2, 4),
+    ((0, 0), (1, 0)),
+    ((0, 1), (0, -1)),
+    ((0, 3), (0, -3)),
+    ((0, 2), (0, -2)),
+    ((1, 1), (1, -1)),
+    ((1, 2), (1, -2)),
+    ((0, 4), (1, -3)),
+    ((1, 4), (1, 3)),
 ]
-TARGETS = sorted({s[:2] for s in FIRST} | {s[:2] for s in THEN if len(s) == 6})
+TARGETS = sorted(
+    {s[:2] for s in FIRST} | {s[:2] for s in THEN if len(s) == 6},
+    key=lambda t: (-abs(t[0]) - t[1], t),
+)
 SENDS = FIRST + [s for s in THEN if len(s) == 6]
 
 
@@ -62,15 +93,23 @@
     sign = 1 - 2 * z
     up, down, across = at(y + sign, z, n_y), at(y - sign, z, n_y), at(y, 1 - z, n_y)
 
+    part = basis_hbm.shape[0] // PIECES
+
     def copy(src, slot_at, to):
-        return pltpu.make_async_remote_copy(
-            src_ref=basis_hbm if src is None else blocks.at[src],
-            dst_ref=blocks.at[slot_at],
-            send_sem=send_sem.at[slot_at],
-            recv_sem=recv_sem.at[slot_at],
-            device_id=(c, to),
-            device_id_type=MESH,
-        )
+        made = []
+        for k in range(PIECES):
+            some = pl.ds(k * part, part)
+            made.append(
+                pltpu.make_async_remote_copy(
+                    src_ref=basis_hbm.at[some] if src is None else blocks.at[src, some],
+                    dst_ref=blocks.at[slot_at, some],
+                    send_sem=send_sem.at[slot_at, k],
+                    recv_sem=recv_sem.at[slot_at, k],
+                    device_id=(c, to),
+                    device_id_type=MESH,
+                )
+            )
+        return made
 
     copies = [
         copy(None, PART, across),
@@ -82,24 +121,29 @@
     ]
 
     def begin():
-        for k in (PART, UP, DOWN):
-            copies[k].start()
+        for k in range(PIECES):
+            for slot_at in (PART, UP, DOWN):
+                copies[slot_at][k].start()
 
     def relay():
-        copies[PART].wait_recv()
-        copies[PART_UP].start()
-        copies[UP].wait_recv()
-        copies[PART_DOWN].start()
+        for k in range(PIECES):
+            copies[PART][k].wait_recv()
+            copies[PART_UP][k].start()
+            copies[UP][k].wait_recv()
+            copies[PART_DOWN][k].start()
 
     def relay_last():
-        copies[PART_DOWN].wait_recv()
-        copies[PART_DOWN2].start()
+        for k in range(PIECES):
+            copies[PART_DOWN][k].wait_recv()
+            copies[PART_DOWN2][k].start()
 
     def finish():
-        for k in (DOWN, PART_UP, PART_DOWN2):
-            copies[k].wait_recv()
-        for k in range(6):
-            copies[k].wait_send()
+        for k in range(PIECES):
+            for slot_at in (DOWN, PART_UP, PART_DOWN2):
+                copies[slot_at][k].wait_recv()
+        for k in range(PIECES):
+            for slot_at in range(6):
+                copies[slot_at][k].wait_send()
 
     return begin, relay, relay_last, finish
 
@@ -145,14 +189,21 @@
 
         return 0
 
-    lax.fori_loop(first_mate, n_clust, greet, 0)
-    for rise, across in TARGETS:
+    def greet_row(rise, across):
         pl.semaphore_signal(
             barrier,
             inc=1,
             device_id=(c, at(y + rise, 1 - z if across else z, n_y)),
             device_id_type=MESH,
         )
+
+    for target in TARGETS:
+        if abs(target[0]) + target[1] >= 2:
+            greet_row(*target)
+    lax.fori_loop(first_mate, n_clust, greet, 0)
+    for target in TARGETS:
+        if abs(target[0]) + target[1] < 2:
+            greet_row(*target)
 
     inter_load.wait()
     inter = inter_ref[...]
@@ -393,8 +444,8 @@
                 pltpu.SemaphoreType.DMA((4,)),
                 pltpu.SemaphoreType.DMA((n_clust,)),
                 pltpu.SemaphoreType.DMA((n_clust,)),
-                pltpu.SemaphoreType.DMA((6,)),
-                pltpu.SemaphoreType.DMA((6,)),
+                pltpu.SemaphoreType.DMA((6, PIECES)),
+                pltpu.SemaphoreType.DMA((6, PIECES)),
                 pltpu.SemaphoreType.DMA((len(SENDS),)),
                 pltpu.SemaphoreType.DMA((len(SENDS),)),
             ],

time: 41.1 us -> 38.4 us (0.934)
  the two profiles are of different devices: /device:TPU:256 before, /device:TPU:384 now
where the time goes in v4:
time: 38.4 us; the launch traced here: 38.2 us
  Pallas kernels  37.5 us (98%)
  between operations  0.66 us (2%)
    pallas_call x1, Pallas kernels, on_device(): pl.pallas_call(gather, out_shape=(jax.ShapeDtypeStruct((n_blk, funcs, col...  36.3 us
    pallas_call x1, Pallas kernels, on_device(): pl.pallas_call(apply_kernel, out_shape=jax.ShapeDtypeStruct((rows, n_blk...  1.26 us

profile of v4, /device:TPU:384, one launch (start us, length us, event | category | flops | bytes accessed | tf_op | source)
XLA Modules:
  0.0 38.2 jit_solution(14319213220663737345)
XLA Ops:
  0.7 36.3 %gather.1 = (bf16[16,256,128]{2,1,0:T(8,128)(2,1)S(1)}, bf16[256,256]{1,0:T(8,128)(2,1)S(1)}) custom-call(bf16[32,8,128]{2,1,0:T(8,128)(2,1)} %refs_0_.1, s32[32,32]{1,0:T(8,128)} %refs_1_.1, bf16[256,256]{1,0:T(8,128)(2,1)} %refs_2_.1, bf16[7,256,256]{2,1,0:T(8,128)(2,1)} %bitcast.1, s32[1]{0:T(128)S(6)} %copy.6.refs_4_), custom_call_target="tpu_custom_call" | custom-call | tf_op jit(solution)/shard_map/gather/pallas_call | solution.py:425
  36.9 1.3 %apply.1 = bf16[256,2048]{1,0:T(8,128)(2,1)} custom-call(bf16[256,256]{1,0:T(8,128)(2,1)S(1)} %get-tuple-element.7.w_ref, bf16[16,256,128]{2,1,0:T(8,128)(2,1)S(1)} %get-tuple-element.8.n_ref), custom_call_target="tpu_custom_call" | custom-call | tf_op jit(solution)/shard_map/apply/pallas_call | solution.py:464

commit v5 on v4

--- a/solution.py
+++ b/solution.py
@@ -14,6 +14,7 @@
 
 GROUPS = 4
 PIECES = 4
+LAST_SENDS = 8
 PARTS = 4
 FIRST = [
     (-1, 0, 0, 0, 0, 2),
@@ -183,10 +184,7 @@
     first_mate, first_later = mine * group, (mine + 1) * group
 
     def greet(to, _):
-        @pl.when(to != c)
-        def _():
-            pl.semaphore_signal(barrier, inc=1, device_id=(to, b), device_id_type=MESH)
-
+        pl.semaphore_signal(barrier, inc=1, device_id=(to, b), device_id_type=MESH)
         return 0
 
     def greet_row(rise, across):
@@ -197,13 +195,22 @@
             device_id_type=MESH,
         )
 
+    def greet_mate(step):
+        to = first_mate + (c - first_mate + step) % group
+        pl.semaphore_signal(barrier, inc=1, device_id=(to, b), device_id_type=MESH)
+
+    middle = sorted(range(1, group), key=lambda step: (abs(step - group // 2), step))
+    for step in middle[:3]:
+        greet_mate(step)
     for target in TARGETS:
         if abs(target[0]) + target[1] >= 2:
             greet_row(*target)
-    lax.fori_loop(first_mate, n_clust, greet, 0)
+    for step in middle[3:]:
+        greet_mate(step)
     for target in TARGETS:
         if abs(target[0]) + target[1] < 2:
             greet_row(*target)
+    lax.fori_loop(first_later, n_clust, greet, 0)
 
     inter_load.wait()
     inter = inter_ref[...]
@@ -339,7 +346,20 @@
         send(k).start()
     k = len(FIRST)
     folded = False
+
+    def a2a_sent(to, _):
+        @pl.when(to != c)
+        def _():
+            a2a(to, c).wait_send()
+
+        return 0
+
     for item in THEN:
+        if item == THEN[-2]:
+            finish_basis()
+            lax.fori_loop(0, n_clust, a2a_sent, 0)
+            for j in range(len(SENDS) - LAST_SENDS):
+                send(j).wait_send()
         if len(item) == 6:
             need(*item[2:])
             send(k).start()
@@ -351,7 +371,6 @@
             term = lax.dot_general(both, both, (((1,), (1,)), ((), ())), preferred_element_type=F32)
             g_ref[...] = g_ref[...] + term if folded else term
             folded = True
-    finish_basis()
 
     basis_load.wait()
     basis = basis_ref[...]
@@ -376,15 +395,7 @@
         w = term if w is None else w + term
     w_out[...] = w.astype(BF16)
 
-    def a2a_sent(to, _):
-        @pl.when(to != c)
-        def _():
-            a2a(to, c).wait_send()
-
-        return 0
-
-    lax.fori_loop(0, n_clust, a2a_sent, 0)
-    for k in range(len(SENDS)):
+    for k in range(len(SENDS) - LAST_SENDS, len(SENDS)):
         send(k).wait_send()
 
 

time: 38.4 us -> 38.1 us (level)
  no operation moved by 1% of the time
where the time goes in v5:
time: 38.1 us; the launch traced here: 37.9 us
  Pallas kernels  37.2 us (98%)
  between operations  0.66 us (2%)
    pallas_call x1, Pallas kernels, on_device(): pl.pallas_call(gather, out_shape=(jax.ShapeDtypeStruct((n_blk, funcs, col...  35.9 us
    pallas_call x1, Pallas kernels, on_device(): pl.pallas_call(apply_kernel, out_shape=jax.ShapeDtypeStruct((rows, n_blk...  1.26 us

profile of v5, /device:TPU:384, one launch (start us, length us, event | category | flops | bytes accessed | tf_op | source)
XLA Modules:
  0.0 37.9 jit_solution(1800333670183638239)
XLA Ops:
  0.7 35.9 %gather.1 = (bf16[16,256,128]{2,1,0:T(8,128)(2,1)S(1)}, bf16[256,256]{1,0:T(8,128)(2,1)S(1)}) custom-call(bf16[32,8,128]{2,1,0:T(8,128)(2,1)} %refs_0_.1, s32[32,32]{1,0:T(8,128)} %refs_1_.1, bf16[256,256]{1,0:T(8,128)(2,1)} %refs_2_.1, bf16[7,256,256]{2,1,0:T(8,128)(2,1)} %bitcast.1, s32[1]{0:T(128)S(6)} %copy.6.refs_4_), custom_call_target="tpu_custom_call" | custom-call | tf_op jit(solution)/shard_map/gather/pallas_call | solution.py:436
  36.6 1.3 %apply.1 = bf16[256,2048]{1,0:T(8,128)(2,1)} custom-call(bf16[256,256]{1,0:T(8,128)(2,1)S(1)} %get-tuple-element.7.w_ref, bf16[16,256,128]{2,1,0:T(8,128)(2,1)S(1)} %get-tuple-element.8.n_ref), custom_call_target="tpu_custom_call" | custom-call | tf_op jit(solution)/shard_map/apply/pallas_call | solution.py:475

commit v6 on v5

--- a/solution.py
+++ b/solution.py
@@ -401,10 +401,10 @@
 
 def apply_kernel(w_ref, n_ref, out_hbm, out_v, sem):
     w = w_ref[...]
-    width = 2 * n_ref.shape[2]
+    width = 4 * n_ref.shape[2]
     copies = []
-    for j in range(n_ref.shape[0] // 2):
-        both = jnp.concatenate([n_ref[2 * j], n_ref[2 * j + 1]], axis=1)
+    for j in range(n_ref.shape[0] // 4):
+        both = jnp.concatenate([n_ref[4 * j + i] for i in range(4)], axis=1)
         where = slice(j * width, (j + 1) * width)
         out_v[:, where] = jnp.dot(w, both, preferred_element_type=F32).astype(BF16)
         copy = pltpu.make_async_copy(out_v.at[:, where], out_hbm.at[:, where], sem.at[j])

time: 38.1 us -> 38.1 us (level)
  no operation moved by 1% of the time
where the time goes in v6:
time: 38.1 us; the launch traced here: 37.9 us
  Pallas kernels  37.2 us (98%)
  between operations  0.66 us (2%)
    pallas_call x1, Pallas kernels, on_device(): pl.pallas_call(gather, out_shape=(jax.ShapeDtypeStruct((n_blk, funcs, col...  35.9 us
    pallas_call x1, Pallas kernels, on_device(): pl.pallas_call(apply_kernel, out_shape=jax.ShapeDtypeStruct((rows, n_blk...  1.27 us

profile of v6, /device:TPU:384, one launch (start us, length us, event | category | flops | bytes accessed | tf_op | source)
XLA Modules:
  0.0 37.9 jit_solution(8520664330377321077)
XLA Ops:
  0.7 35.9 %gather.1 = (bf16[16,256,128]{2,1,0:T(8,128)(2,1)S(1)}, bf16[256,256]{1,0:T(8,128)(2,1)S(1)}) custom-call(bf16[32,8,128]{2,1,0:T(8,128)(2,1)} %refs_0_.1, s32[32,32]{1,0:T(8,128)} %refs_1_.1, bf16[256,256]{1,0:T(8,128)(2,1)} %refs_2_.1, bf16[7,256,256]{2,1,0:T(8,128)(2,1)} %bitcast.1, s32[1]{0:T(128)S(6)} %copy.6.refs_4_), custom_call_target="tpu_custom_call" | custom-call | tf_op jit(solution)/shard_map/gather/pallas_call | solution.py:436
  36.6 1.3 %apply.1 = bf16[256,2048]{1,0:T(8,128)(2,1)} custom-call(bf16[256,256]{1,0:T(8,128)(2,1)S(1)} %get-tuple-element.7.w_ref, bf16[16,256,128]{2,1,0:T(8,128)(2,1)S(1)} %get-tuple-element.8.n_ref), custom_call_target="tpu_custom_call" | custom-call | tf_op jit(solution)/shard_map/apply/pallas_call | solution.py:475
